TPU v7x, 32 devices: a whole 2x2x4 slice. The times are simulated.
32 devices in a mesh: member: 2 (over x), space: 8 (over z, y), cuts: 2 (over core).
Axes of the slice: x: 2, y: 2, z: 4, core: 2. Of those that a mesh axis runs over, the one named last changes fastest.
Arguments:
- depth_class: int32 [64, 2048], P('space'), may hold values from 0 to 7
- coef_table: float32 [2, 8], replicated, may hold values from 0.3 to 2
- step_counts: int32 [2], replicated, may hold values from 9 to 12, as said below
- closure_weights: float32 [18, 3, 3], P('member'), parts along dimension 0, may hold values from -1.25 to 1.25
- checkpoints: float32 [4, 3, 64, 2048], P(('member', 'cuts'), None, 'space'), parts along dimension 0, may hold values from -6 to 6
- old_adjoint: float32 [4, 3, 64, 2048], P(('member', 'cuts'), None, 'space'), parts along dimension 0, may hold values from -6 to 6
Outputs:
- new_adjoint: float32 [4, 3, 64, 2048], P(('member', 'cuts'), None, 'space'), parts along dimension 0
- closure_grad: float32 [18, 3, 3], P('member'), parts along dimension 0
There are 2 independent parts, one for each index of `member`. A program takes and returns all parts, laid end to end along the dimension named above; an argument that names none is the same for every part. Nothing has to cross between parts.
Inputs may be any that keep to these rules, and one draw needn't show every extreme that they name: `step_counts`: some slice takes exactly 12 steps.
All inputs are finite; a program needn't handle non-finite values.
Results may differ from a plain program's by a relative error of at most 0.00026.
Values sent between devices are 32-bit elements; how exact they have to be, the bound alone decides.
A program may use at most 128 MiB of HBM per device.

v0:
```python
import jax
import jax.numpy as jnp
from jax import lax
from jax.sharding import PartitionSpec as P

FINE = 12


fine_rate = 0.05
highest = lax.Precision.HIGHEST


def with_halo(cells, sides, width):
    for axis, dim in sides:
        count = lax.axis_size(axis)
        ends = count - 1
        head = lax.slice_in_dim(cells, 0, width, axis=dim)
        tail = lax.slice_in_dim(cells, cells.shape[dim] - width, cells.shape[dim], axis=dim)
        cells = jnp.concatenate(
            [
                lax.ppermute(tail, axis, [(i, (i + 1) % count) for i in range(ends)]),
                cells,
                lax.ppermute(head, axis, [((i + 1) % count, i) for i in range(ends)]),
            ],
            axis=dim,
        )
    return cells


def shifted_2(array, axis, by):
    devices = lax.axis_size(axis)
    pairs = [(i, i + by) for i in range(devices) if 0 <= i + by < devices]
    return lax.ppermute(array, axis, pairs)


def offset_view(widened, offset_row, offset_col, row_count, col_count):
    return widened[
        :, 1 + offset_row : 1 + offset_row + row_count, 1 + offset_col : 1 + offset_col + col_count
    ]


def advance(padded, depth_field, friction, weights, step_rate):
    row_count = padded.shape[1] - 2
    col_count = padded.shape[2]
    widened = jnp.pad(padded, ((0, 0), (0, 0), (1, 1)))
    centre = offset_view(widened, 0, 0, row_count, col_count)
    to_east = offset_view(widened, 0, 1, row_count, col_count)
    to_west = offset_view(widened, 0, -1, row_count, col_count)
    to_north = offset_view(widened, 1, 0, row_count, col_count)
    to_south = offset_view(widened, -1, 0, row_count, col_count)
    spread = 0.5 * (to_east[1] - to_west[1] + (to_north[2] - to_south[2]))
    height = centre[0] - step_rate * depth_field * spread
    along_x = centre[1] - step_rate * (0.5 * (to_east[0] - to_west[0]) + friction * centre[1])
    along_y = centre[2] - step_rate * (0.5 * (to_north[0] - to_south[0]) + friction * centre[2])
    closure = jnp.zeros_like(centre)
    for offset_row in (-1, 0, 1):
        for offset_col in (-1, 0, 1):
            stencil_index = 3 * (offset_row + 1) + offset_col + 1
            closure = closure + jnp.einsum(
                "oc,cij->oij",
                weights[stencil_index],
                offset_view(widened, offset_row, offset_col, row_count, col_count),
                precision=highest,
            )
    return jnp.stack([height, along_x, along_y]) + step_rate * closure


def pull_back(cotangent, depth_field, friction, weights, step_rate):
    inner_rows = cotangent.shape[1] - 2

    def forward(inner_state):
        return advance(
            jnp.pad(inner_state, ((0, 0), (2, 2), (0, 0))),
            depth_field,
            friction,
            weights,
            step_rate,
        )

    _, pullback = jax.vjp(
        forward, jnp.zeros((cotangent.shape[0], inner_rows, cotangent.shape[2]), jnp.float32)
    )
    return pullback(cotangent)[0]


def closure_terms(adjoint, padded, step_rate):
    row_count = adjoint.shape[1]
    col_count = adjoint.shape[2]
    widened = jnp.pad(padded, ((0, 0), (0, 0), (1, 1)))
    terms = []
    for offset_row in (-1, 0, 1):
        for offset_col in (-1, 0, 1):
            shifted = offset_view(widened, offset_row, offset_col, row_count, col_count)
            terms.append(jnp.einsum("oij,cij->oc", adjoint, shifted, precision=highest))
    return step_rate * jnp.stack(terms)


def body(depth_class, coef_table, step_counts, closure_weights, checkpoints, old_adjoint):
    row_count = depth_class.shape[0]
    col_count = depth_class.shape[1]
    classes = coef_table.shape[1]
    strips = lax.axis_size("space")
    slice_count = lax.axis_size("cuts")
    matches = (
        depth_class[None, :, :] == jnp.arange(classes, dtype=jnp.int32)[:, None, None]
    ).astype(jnp.float32)
    coefficients = jnp.einsum("jk,kab->jab", coef_table, matches, precision=highest)
    margin = 1
    coef_pad = with_halo(coefficients, (("space", 1),), margin)
    step_total = lax.dynamic_index_in_dim(step_counts, lax.axis_index("cuts"), keepdims=False)

    def coef_rows(rim_width):
        trimmed = coef_pad[:, margin - rim_width : margin + row_count + rim_width]
        return (trimmed[0], trimmed[1])

    def forward_block(state_now, block_index):
        stored = []
        for inner_step in range(4):
            padded = with_halo(state_now, (("space", 1),), 1)
            stored.append(padded)
            depth_field, friction = coef_rows(0)
            stepped = advance(padded, depth_field, friction, closure_weights, fine_rate)
            active = block_index * 4 + inner_step < step_total
            state_now = jnp.where(active, stepped, state_now)
        return (state_now, stored)

    def first_pass(state_now, block_index):
        state_next, stored = forward_block(state_now, block_index)
        return (state_next, state_now)

    block_numbers = jnp.arange(FINE // 4, dtype=jnp.int32)
    _, saved_blocks = lax.scan(first_pass, checkpoints[0], block_numbers)

    def adjoint_block(carried, inputs):
        adjoint, gradient = carried
        block_index, saved = inputs
        _, stored = forward_block(saved, block_index)
        for inner_step in reversed(range(4)):
            active = block_index * 4 + inner_step < step_total
            gradient = gradient + jnp.where(
                active, closure_terms(adjoint, stored[inner_step], fine_rate), 0.0
            )
            padded = with_halo(adjoint, (("space", 1),), 1)
            depth_field, friction = coef_rows(1)
            pulled = pull_back(padded, depth_field, friction, closure_weights, fine_rate)
            adjoint = jnp.where(active, pulled, adjoint)
        return ((adjoint, gradient), None)

    initial = (old_adjoint[0], jnp.zeros((9, 3, 3), jnp.float32))
    (fine_start, gradient), _ = lax.scan(
        adjoint_block, initial, (block_numbers, saved_blocks), reverse=True
    )
    coarse_rate = step_total.astype(jnp.float32) * fine_rate

    def coarse_back(field):
        padded = with_halo(field, (("space", 1),), 1)
        depth_field, friction = coef_rows(1)
        return pull_back(padded, depth_field, friction, closure_weights, coarse_rate)

    previous = old_adjoint[0]
    difference = fine_start - coarse_back(previous)
    last_slice = lax.axis_index("cuts") == slice_count - 1
    ending = previous
    beginning = previous
    for turn_index in range(slice_count):
        beginning = coarse_back(ending) + difference
        if turn_index + 1 < slice_count:
            arrived = shifted_2(beginning, "cuts", -1)
            ending = jnp.where(last_slice, previous, arrived)
    gradient_sum = lax.psum(gradient, ("space", "cuts"))
    grad_scale = float(row_count * strips * col_count * slice_count) ** (-0.5)
    return (beginning[None], gradient_sum * grad_scale)


def solution(mesh):
    return jax.shard_map(
        body,
        mesh=mesh,
        in_specs=(
            P("space", None),
            P(),
            P(),
            P("member", None, None),
            P(("member", "cuts"), None, "space", None),
            P(("member", "cuts"), None, "space", None),
        ),
        out_specs=(P(("member", "cuts"), None, "space", None), P("member", None, None)),
        check_vma=False,
    )
```

profile of v0, /device:TPU:0, one launch (start us, length us, event | category | flops | bytes accessed | tf_op | source)
XLA Modules:
  0.0 999.5 jit_solution(15971986889529123791)
XLA Ops:
  3.2 5.5 collective-permute-start.26
  10.2 5.5 collective-permute-start.24
  32.4 241.4 %while.32 = (s32[]{:T(128)}, f32[3,8,2048]{2,1,0:T(8,128)S(1)}, f32[3,3,8,2048]{3,2,1,0:T(8,128)}, s32[3]{0:T(128)S(1)}, s32[]{:T(128)}, /*index=5*/f32[2,8,2048...) while((s32[]{:T(128)}, f32[3,8,2048]{2,1,0:T(8,128)S(1)}, ...), condition=%wide.region_1.2_spmd, body=%wide.region_0.1_spmd.sunk | while | flops 70043520 | bytes 43853292 | solution.py:132
  54.4 4.8 collective-permute-start
  76.9 4.5 collective-permute-start.2
  83.5 4.2 collective-permute-done.3
  94.9 4.8 collective-permute-start.4
  101.7 3.7 collective-permute-done.5
  112.7 2.9 collective-permute-start.6
  117.6 3.7 collective-permute-done.7
  128.6 4.8 collective-permute-start
  151.2 4.5 collective-permute-start.2
  157.7 3.7 collective-permute-done.3
  168.7 3.8 collective-permute-start.4
  174.5 3.7 collective-permute-done.5
  185.5 3.9 collective-permute-start.6
  191.4 3.7 collective-permute-done.7
  202.4 3.7 collective-permute-start
  223.8 4.5 collective-permute-start.2
  230.4 3.7 collective-permute-done.3
  241.4 3.7 collective-permute-start.4
  247.1 3.9 collective-permute-done.5
  258.2 2.7 collective-permute-start.6
  262.9 3.7 collective-permute-done.7
  273.8 671.4 %while.33 = (s32[]{:T(128)}, f32[3,8,2048]{2,1,0:T(8,128)S(1)}, f32[9,3,3]{0,2,1:T(4,128)}, s32[3]{0:T(128)S(1)}, s32[]{:T(128)}, /*index=5*/f32[9,3,3]{2,1,0:T(...) while((s32[]{:T(128)}, f32[3,8,2048]{2,1,0:T(8,128)S(1)}, ...), condition=%wide.region_3.4_spmd.clone, body=%wide.region_2.3_spmd.clone.sunk | while | flops 204624768 | bytes 137333520 | solution.py:150
  283.6 4.5 collective-permute-start.9
  290.5 4.5 collective-permute-start.17
  311.0 5.5 collective-permute-start.11
  323.5 2.0 fusion.1455
  327.5 5.9 collective-permute-start.19
  369.0 5.4 collective-permute-start.13
  378.6 5.4 collective-permute-start.21
  413.5 2.0 convolution_bitcast_fusion.117
  421.5 2.2 convolution_bitcast_fusion.114
  435.0 5.4 collective-permute-start.15
  453.6 5.9 collective-permute-start.23
  495.8 2.2 pad_add_fusion.88
  500.5 5.4 collective-permute-start.9
  508.2 5.4 collective-permute-start.17
  529.7 5.9 collective-permute-start.11
  542.6 2.0 fusion.1455
  546.6 5.6 collective-permute-start.19
  587.9 5.4 collective-permute-start.13
  597.4 5.5 collective-permute-start.21
  632.5 2.0 convolution_bitcast_fusion.117
  640.6 2.1 convolution_bitcast_fusion.114
  654.0 5.4 collective-permute-start.15
  672.7 5.7 collective-permute-start.23
  714.9 2.2 pad_add_fusion.88
  719.5 5.4 collective-permute-start.9
  727.2 5.4 collective-permute-start.17
  748.7 5.7 collective-permute-start.11
  761.4 2.0 fusion.1455
  765.4 5.9 collective-permute-start.19
  806.9 5.4 collective-permute-start.13
  816.4 5.4 collective-permute-start.21
  851.3 2.0 convolution_bitcast_fusion.117
  859.4 2.2 convolution_bitcast_fusion.114
  872.9 5.4 collective-permute-start.15
  891.5 5.9 collective-permute-start.23
  933.7 2.2 pad_add_fusion.88
  945.2 2.1 fusion.594
  948.6 31.1 %psum.7 = f32[9,3,3]{0,2,1:T(4,128)S(1)} all-reduce(f32[9,3,3]{0,2,1:T(4,128)S(1)} %copy-done.38), channel_id=1, replica_groups=mesh['member'=2,'space'=8,'cuts'=2] {'space','cuts'}, use_global_device_ids=true, to_apply=%region_4.5 | all-reduce | flops 81 | bytes 648 | tf_op jit(solution)/shard_map/psum | solution.py:170
  981.3 4.5 collective-permute-start.29
  (1362 shorter events, 644.9 us)
Async XLA Ops:
  1.9 16.3 %collective-permute-start.27 = (f32[2,1,2048]{2,0,1:T(2,128)S(1)}, f32[2,1,2048]{2,0,1:T(2,128)S(1)}, u32[]{:S(2)}, u32[]{:S(2)}) collective-permute-start(f32[2,1,2048]{2,0,1:T(2,128)S(1)} %get-tuple-element.691), channel_id=1, source_target_pairs={{2,0},{4,2},{6,4},{8,6},{10,8},{12,10},{14,12},{3,1},{5,3},{7,5},{... | collective-permute-start | bytes 49160 | tf_op jit(solution)/shard_map/ppermute | solution.py:23
  3.2 15.0 %collective-permute-start.26 = (f32[2,1,2048]{2,0,1:T(2,128)S(1)}, f32[2,1,2048]{2,0,1:T(2,128)S(1)}, u32[]{:S(2)}, u32[]{:S(2)}) collective-permute-start(f32[2,1,2048]{2,0,1:T(2,128)S(1)} %get-tuple-element.690), channel_id=1, source_target_pairs={{0,2},{2,4},{4,6},{6,8},{8,10},{10,12},{12,14},{1,3},{3,5},{5,7},{... | collective-permute-start | bytes 49160 | tf_op jit(solution)/shard_map/ppermute | solution.py:21
  8.9 9.6 collective-permute-start.25
  10.2 8.3 collective-permute-start.24
  54.4 11.0 %collective-permute-start = (f32[3,1,2048]{2,1,0:T(1,128)S(1)}, f32[3,1,2048]{2,1,0:T(1,128)S(1)}, u32[]{:S(2)}, u32[]{:S(2)}) collective-permute-start(f32[3,1,2048]{2,1,0:T(1,128)S(1)} %get-tuple-element.971), channel_id=1, source_target_pairs={{0,2},{2,4},{4,6},{6,8},{8,10},{10,12},{12,14},{1,3},{3,5},{5,7},{... | collective-permute-start | bytes 73736 | tf_op jit(solution)/shard_map/while/body/eval_jaxpr/ppermute | solution.py:21
  59.2 6.2 collective-permute-start.1
  76.9 6.5 collective-permute-start.2
  94.9 6.8 collective-permute-start.4
  128.6 11.0 %collective-permute-start = (f32[3,1,2048]{2,1,0:T(1,128)S(1)}, f32[3,1,2048]{2,1,0:T(1,128)S(1)}, u32[]{:S(2)}, u32[]{:S(2)}) collective-permute-start(f32[3,1,2048]{2,1,0:T(1,128)S(1)} %get-tuple-element.971), channel_id=1, source_target_pairs={{0,2},{2,4},{4,6},{6,8},{8,10},{10,12},{12,14},{1,3},{3,5},{5,7},{... | collective-permute-start | bytes 73736 | tf_op jit(solution)/shard_map/while/body/eval_jaxpr/ppermute | solution.py:21
  133.4 6.2 collective-permute-start.1
  151.2 6.5 collective-permute-start.2
  202.4 9.9 collective-permute-start
  206.1 6.2 collective-permute-start.1
  223.8 6.5 collective-permute-start.2
  282.3 17.1 %collective-permute-start.8 = (f32[3,1,2048]{2,1,0:T(1,128)S(1)}, f32[3,1,2048]{2,1,0:T(1,128)S(1)}, u32[]{:S(2)}, u32[]{:S(2)}) collective-permute-start(f32[3,1,2048]{2,1,0:T(1,128)S(1)} %get-tuple-element.1032), channel_id=1, source_target_pairs={{2,0},{4,2},{6,4},{8,6},{10,8},{12,10},{14,12},{3,1},{5,3},{7,5},{... | collective-permute-start | bytes 73736 | tf_op jit(solution)/shard_map/while/body/eval_jaxpr/ppermute | solution.py:23
  283.6 15.8 %collective-permute-start.9 = (f32[3,1,2048]{2,1,0:T(1,128)S(1)}, f32[3,1,2048]{2,1,0:T(1,128)S(1)}, u32[]{:S(2)}, u32[]{:S(2)}) collective-permute-start(f32[3,1,2048]{2,1,0:T(1,128)S(1)} %get-tuple-element.1033), channel_id=1, source_target_pairs={{0,2},{2,4},{4,6},{6,8},{8,10},{10,12},{12,14},{1,3},{3,5},{5,7},{... | collective-permute-start | bytes 73736 | tf_op jit(solution)/shard_map/while/body/eval_jaxpr/ppermute | solution.py:21
  289.2 27.3 %collective-permute-start.16 = (f32[3,1,2048]{2,1,0:T(1,128)S(1)}, f32[3,1,2048]{2,1,0:T(1,128)S(1)}, u32[]{:S(2)}, u32[]{:S(2)}) collective-permute-start(f32[3,1,2048]{2,1,0:T(1,128)S(1)} %get-tuple-element.1112), channel_id=1, source_target_pairs={{2,0},{4,2},{6,4},{8,6},{10,8},{12,10},{14,12},{3,1},{5,3},{7,5},{... | collective-permute-start | bytes 73736 | tf_op jit(solution)/shard_map/while/body/eval_jaxpr/ppermute | solution.py:23
  290.5 26.0 %collective-permute-start.17 = (f32[3,1,2048]{2,1,0:T(1,128)S(1)}, f32[3,1,2048]{2,1,0:T(1,128)S(1)}, u32[]{:S(2)}, u32[]{:S(2)}) collective-permute-start(f32[3,1,2048]{2,1,0:T(1,128)S(1)} %get-tuple-element.1113), channel_id=1, source_target_pairs={{0,2},{2,4},{4,6},{6,8},{8,10},{10,12},{12,14},{1,3},{3,5},{5,7},{... | collective-permute-start | bytes 73736 | tf_op jit(solution)/shard_map/while/body/eval_jaxpr/ppermute | solution.py:21
  309.7 23.7 %collective-permute-start.10 = (f32[3,1,2048]{2,1,0:T(1,128)S(1)}, f32[3,1,2048]{2,1,0:T(1,128)S(1)}, u32[]{:S(2)}, u32[]{:S(2)}) collective-permute-start(f32[3,1,2048]{2,1,0:T(1,128)S(1)} %get-tuple-element.1058), channel_id=1, source_target_pairs={{2,0},{4,2},{6,4},{8,6},{10,8},{12,10},{14,12},{3,1},{5,3},{7,5},{... | collective-permute-start | bytes 73736 | tf_op jit(solution)/shard_map/while/body/eval_jaxpr/ppermute | solution.py:23
  311.0 22.4 %collective-permute-start.11 = (f32[3,1,2048]{2,1,0:T(1,128)S(1)}, f32[3,1,2048]{2,1,0:T(1,128)S(1)}, u32[]{:S(2)}, u32[]{:S(2)}) collective-permute-start(f32[3,1,2048]{2,1,0:T(1,128)S(1)} %get-tuple-element.1059), channel_id=1, source_target_pairs={{0,2},{2,4},{4,6},{6,8},{8,10},{10,12},{12,14},{1,3},{3,5},{5,7},{... | collective-permute-start | bytes 73736 | tf_op jit(solution)/shard_map/while/body/eval_jaxpr/ppermute | solution.py:21
  326.2 19.5 %collective-permute-start.18 = (f32[3,1,2048]{2,1,0:T(1,128)S(1)}, f32[3,1,2048]{2,1,0:T(1,128)S(1)}, u32[]{:S(2)}, u32[]{:S(2)}) collective-permute-start(f32[3,1,2048]{2,1,0:T(1,128)S(1)} %get-tuple-element.1125), channel_id=1, source_target_pairs={{2,0},{4,2},{6,4},{8,6},{10,8},{12,10},{14,12},{3,1},{5,3},{7,5},{... | collective-permute-start | bytes 73736 | tf_op jit(solution)/shard_map/while/body/eval_jaxpr/ppermute | solution.py:23
  327.5 18.2 %collective-permute-start.19 = (f32[3,1,2048]{2,1,0:T(1,128)S(1)}, f32[3,1,2048]{2,1,0:T(1,128)S(1)}, u32[]{:S(2)}, u32[]{:S(2)}) collective-permute-start(f32[3,1,2048]{2,1,0:T(1,128)S(1)} %get-tuple-element.1126), channel_id=1, source_target_pairs={{0,2},{2,4},{4,6},{6,8},{8,10},{10,12},{12,14},{1,3},{3,5},{5,7},{... | collective-permute-start | bytes 73736 | tf_op jit(solution)/shard_map/while/body/eval_jaxpr/ppermute | solution.py:21
  367.7 17.7 %collective-permute-start.12 = (f32[3,1,2048]{2,1,0:T(1,128)}, f32[3,1,2048]{2,1,0:T(1,128)S(1)}, u32[]{:S(2)}, u32[]{:S(2)}) collective-permute-start(f32[3,1,2048]{2,1,0:T(1,128)} %get-tuple-element.1076), channel_id=1, source_target_pairs={{2,0},{4,2},{6,4},{8,6},{10,8},{12,10},{14,12},{3,1},{5,3},{7,5},{... | collective-permute-start | bytes 73736 | tf_op jit(solution)/shard_map/while/body/eval_jaxpr/ppermute | solution.py:23
  369.0 16.4 %collective-permute-start.13 = (f32[3,1,2048]{2,1,0:T(1,128)S(1)}, f32[3,1,2048]{2,1,0:T(1,128)S(1)}, u32[]{:S(2)}, u32[]{:S(2)}) collective-permute-start(f32[3,1,2048]{2,1,0:T(1,128)S(1)} %get-tuple-element.1077), channel_id=1, source_target_pairs={{0,2},{2,4},{4,6},{6,8},{8,10},{10,12},{12,14},{1,3},{3,5},{5,7},{... | collective-permute-start | bytes 73736 | tf_op jit(solution)/shard_map/while/body/eval_jaxpr/ppermute | solution.py:21
  377.3 35.7 %collective-permute-start.20 = (f32[3,1,2048]{2,1,0:T(1,128)S(1)}, f32[3,1,2048]{2,1,0:T(1,128)S(1)}, u32[]{:S(2)}, u32[]{:S(2)}) collective-permute-start(f32[3,1,2048]{2,1,0:T(1,128)S(1)} %get-tuple-element.1138), channel_id=1, source_target_pairs={{2,0},{4,2},{6,4},{8,6},{10,8},{12,10},{14,12},{3,1},{5,3},{7,5},{... | collective-permute-start | bytes 73736 | tf_op jit(solution)/shard_map/while/body/eval_jaxpr/ppermute | solution.py:23
  378.6 34.4 %collective-permute-start.21 = (f32[3,1,2048]{2,1,0:T(1,128)S(1)}, f32[3,1,2048]{2,1,0:T(1,128)S(1)}, u32[]{:S(2)}, u32[]{:S(2)}) collective-permute-start(f32[3,1,2048]{2,1,0:T(1,128)S(1)} %get-tuple-element.1139), channel_id=1, source_target_pairs={{0,2},{2,4},{4,6},{6,8},{8,10},{10,12},{12,14},{1,3},{3,5},{5,7},{... | collective-permute-start | bytes 73736 | tf_op jit(solution)/shard_map/while/body/eval_jaxpr/ppermute | solution.py:21
  433.7 27.9 %collective-permute-start.14 = (f32[3,1,2048]{2,1,0:T(1,128)}, f32[3,1,2048]{2,1,0:T(1,128)S(1)}, u32[]{:S(2)}, u32[]{:S(2)}) collective-permute-start(f32[3,1,2048]{2,1,0:T(1,128)} %get-tuple-element.1094), channel_id=1, source_target_pairs={{2,0},{4,2},{6,4},{8,6},{10,8},{12,10},{14,12},{3,1},{5,3},{7,5},{... | collective-permute-start | bytes 73736 | tf_op jit(solution)/shard_map/while/body/eval_jaxpr/ppermute | solution.py:23
  435.0 26.6 %collective-permute-start.15 = (f32[3,1,2048]{2,1,0:T(1,128)}, f32[3,1,2048]{2,1,0:T(1,128)S(1)}, u32[]{:S(2)}, u32[]{:S(2)}) collective-permute-start(f32[3,1,2048]{2,1,0:T(1,128)} %get-tuple-element.1095), channel_id=1, source_target_pairs={{0,2},{2,4},{4,6},{6,8},{8,10},{10,12},{12,14},{1,3},{3,5},{5,7},{... | collective-permute-start | bytes 73736 | tf_op jit(solution)/shard_map/while/body/eval_jaxpr/ppermute | solution.py:21
  452.4 24.2 %collective-permute-start.22 = (f32[3,1,2048]{2,1,0:T(1,128)S(1)}, f32[3,1,2048]{2,1,0:T(1,128)S(1)}, u32[]{:S(2)}, u32[]{:S(2)}) collective-permute-start(f32[3,1,2048]{2,1,0:T(1,128)S(1)} %get-tuple-element.1151), channel_id=1, source_target_pairs={{2,0},{4,2},{6,4},{8,6},{10,8},{12,10},{14,12},{3,1},{5,3},{7,5},{... | collective-permute-start | bytes 73736 | tf_op jit(solution)/shard_map/while/body/eval_jaxpr/ppermute | solution.py:23
  453.6 22.9 %collective-permute-start.23 = (f32[3,1,2048]{2,1,0:T(1,128)S(1)}, f32[3,1,2048]{2,1,0:T(1,128)S(1)}, u32[]{:S(2)}, u32[]{:S(2)}) collective-permute-start(f32[3,1,2048]{2,1,0:T(1,128)S(1)} %get-tuple-element.1152), channel_id=1, source_target_pairs={{0,2},{2,4},{4,6},{6,8},{8,10},{10,12},{12,14},{1,3},{3,5},{5,7},{... | collective-permute-start | bytes 73736 | tf_op jit(solution)/shard_map/while/body/eval_jaxpr/ppermute | solution.py:21
  499.2 18.9 %collective-permute-start.8 = (f32[3,1,2048]{2,1,0:T(1,128)S(1)}, f32[3,1,2048]{2,1,0:T(1,128)S(1)}, u32[]{:S(2)}, u32[]{:S(2)}) collective-permute-start(f32[3,1,2048]{2,1,0:T(1,128)S(1)} %get-tuple-element.1032), channel_id=1, source_target_pairs={{2,0},{4,2},{6,4},{8,6},{10,8},{12,10},{14,12},{3,1},{5,3},{7,5},{... | collective-permute-start | bytes 73736 | tf_op jit(solution)/shard_map/while/body/eval_jaxpr/ppermute | solution.py:23
  500.5 17.6 %collective-permute-start.9 = (f32[3,1,2048]{2,1,0:T(1,128)S(1)}, f32[3,1,2048]{2,1,0:T(1,128)S(1)}, u32[]{:S(2)}, u32[]{:S(2)}) collective-permute-start(f32[3,1,2048]{2,1,0:T(1,128)S(1)} %get-tuple-element.1033), channel_id=1, source_target_pairs={{0,2},{2,4},{4,6},{6,8},{8,10},{10,12},{12,14},{1,3},{3,5},{5,7},{... | collective-permute-start | bytes 73736 | tf_op jit(solution)/shard_map/while/body/eval_jaxpr/ppermute | solution.py:21
  506.9 28.6 %collective-permute-start.16 = (f32[3,1,2048]{2,1,0:T(1,128)S(1)}, f32[3,1,2048]{2,1,0:T(1,128)S(1)}, u32[]{:S(2)}, u32[]{:S(2)}) collective-permute-start(f32[3,1,2048]{2,1,0:T(1,128)S(1)} %get-tuple-element.1112), channel_id=1, source_target_pairs={{2,0},{4,2},{6,4},{8,6},{10,8},{12,10},{14,12},{3,1},{5,3},{7,5},{... | collective-permute-start | bytes 73736 | tf_op jit(solution)/shard_map/while/body/eval_jaxpr/ppermute | solution.py:23
  508.2 27.3 %collective-permute-start.17 = (f32[3,1,2048]{2,1,0:T(1,128)S(1)}, f32[3,1,2048]{2,1,0:T(1,128)S(1)}, u32[]{:S(2)}, u32[]{:S(2)}) collective-permute-start(f32[3,1,2048]{2,1,0:T(1,128)S(1)} %get-tuple-element.1113), channel_id=1, source_target_pairs={{0,2},{2,4},{4,6},{6,8},{8,10},{10,12},{12,14},{1,3},{3,5},{5,7},{... | collective-permute-start | bytes 73736 | tf_op jit(solution)/shard_map/while/body/eval_jaxpr/ppermute | solution.py:21
  528.4 23.9 %collective-permute-start.10 = (f32[3,1,2048]{2,1,0:T(1,128)S(1)}, f32[3,1,2048]{2,1,0:T(1,128)S(1)}, u32[]{:S(2)}, u32[]{:S(2)}) collective-permute-start(f32[3,1,2048]{2,1,0:T(1,128)S(1)} %get-tuple-element.1058), channel_id=1, source_target_pairs={{2,0},{4,2},{6,4},{8,6},{10,8},{12,10},{14,12},{3,1},{5,3},{7,5},{... | collective-permute-start | bytes 73736 | tf_op jit(solution)/shard_map/while/body/eval_jaxpr/ppermute | solution.py:23
  529.7 22.6 %collective-permute-start.11 = (f32[3,1,2048]{2,1,0:T(1,128)S(1)}, f32[3,1,2048]{2,1,0:T(1,128)S(1)}, u32[]{:S(2)}, u32[]{:S(2)}) collective-permute-start(f32[3,1,2048]{2,1,0:T(1,128)S(1)} %get-tuple-element.1059), channel_id=1, source_target_pairs={{0,2},{2,4},{4,6},{6,8},{8,10},{10,12},{12,14},{1,3},{3,5},{5,7},{... | collective-permute-start | bytes 73736 | tf_op jit(solution)/shard_map/while/body/eval_jaxpr/ppermute | solution.py:21
  545.3 19.2 %collective-permute-start.18 = (f32[3,1,2048]{2,1,0:T(1,128)S(1)}, f32[3,1,2048]{2,1,0:T(1,128)S(1)}, u32[]{:S(2)}, u32[]{:S(2)}) collective-permute-start(f32[3,1,2048]{2,1,0:T(1,128)S(1)} %get-tuple-element.1125), channel_id=1, source_target_pairs={{2,0},{4,2},{6,4},{8,6},{10,8},{12,10},{14,12},{3,1},{5,3},{7,5},{... | collective-permute-start | bytes 73736 | tf_op jit(solution)/shard_map/while/body/eval_jaxpr/ppermute | solution.py:23
  546.6 17.9 %collective-permute-start.19 = (f32[3,1,2048]{2,1,0:T(1,128)S(1)}, f32[3,1,2048]{2,1,0:T(1,128)S(1)}, u32[]{:S(2)}, u32[]{:S(2)}) collective-permute-start(f32[3,1,2048]{2,1,0:T(1,128)S(1)} %get-tuple-element.1126), channel_id=1, source_target_pairs={{0,2},{2,4},{4,6},{6,8},{8,10},{10,12},{12,14},{1,3},{3,5},{5,7},{... | collective-permute-start | bytes 73736 | tf_op jit(solution)/shard_map/while/body/eval_jaxpr/ppermute | solution.py:21
  586.6 17.7 %collective-permute-start.12 = (f32[3,1,2048]{2,1,0:T(1,128)}, f32[3,1,2048]{2,1,0:T(1,128)S(1)}, u32[]{:S(2)}, u32[]{:S(2)}) collective-permute-start(f32[3,1,2048]{2,1,0:T(1,128)} %get-tuple-element.1076), channel_id=1, source_target_pairs={{2,0},{4,2},{6,4},{8,6},{10,8},{12,10},{14,12},{3,1},{5,3},{7,5},{... | collective-permute-start | bytes 73736 | tf_op jit(solution)/shard_map/while/body/eval_jaxpr/ppermute | solution.py:23
  587.9 16.4 %collective-permute-start.13 = (f32[3,1,2048]{2,1,0:T(1,128)S(1)}, f32[3,1,2048]{2,1,0:T(1,128)S(1)}, u32[]{:S(2)}, u32[]{:S(2)}) collective-permute-start(f32[3,1,2048]{2,1,0:T(1,128)S(1)} %get-tuple-element.1077), channel_id=1, source_target_pairs={{0,2},{2,4},{4,6},{6,8},{8,10},{10,12},{12,14},{1,3},{3,5},{5,7},{... | collective-permute-start | bytes 73736 | tf_op jit(solution)/shard_map/while/body/eval_jaxpr/ppermute | solution.py:21
  596.1 35.9 %collective-permute-start.20 = (f32[3,1,2048]{2,1,0:T(1,128)S(1)}, f32[3,1,2048]{2,1,0:T(1,128)S(1)}, u32[]{:S(2)}, u32[]{:S(2)}) collective-permute-start(f32[3,1,2048]{2,1,0:T(1,128)S(1)} %get-tuple-element.1138), channel_id=1, source_target_pairs={{2,0},{4,2},{6,4},{8,6},{10,8},{12,10},{14,12},{3,1},{5,3},{7,5},{... | collective-permute-start | bytes 73736 | tf_op jit(solution)/shard_map/while/body/eval_jaxpr/ppermute | solution.py:23
  597.4 34.6 %collective-permute-start.21 = (f32[3,1,2048]{2,1,0:T(1,128)S(1)}, f32[3,1,2048]{2,1,0:T(1,128)S(1)}, u32[]{:S(2)}, u32[]{:S(2)}) collective-permute-start(f32[3,1,2048]{2,1,0:T(1,128)S(1)} %get-tuple-element.1139), channel_id=1, source_target_pairs={{0,2},{2,4},{4,6},{6,8},{8,10},{10,12},{12,14},{1,3},{3,5},{5,7},{... | collective-permute-start | bytes 73736 | tf_op jit(solution)/shard_map/while/body/eval_jaxpr/ppermute | solution.py:21
  652.7 27.7 %collective-permute-start.14 = (f32[3,1,2048]{2,1,0:T(1,128)}, f32[3,1,2048]{2,1,0:T(1,128)S(1)}, u32[]{:S(2)}, u32[]{:S(2)}) collective-permute-start(f32[3,1,2048]{2,1,0:T(1,128)} %get-tuple-element.1094), channel_id=1, source_target_pairs={{2,0},{4,2},{6,4},{8,6},{10,8},{12,10},{14,12},{3,1},{5,3},{7,5},{... | collective-permute-start | bytes 73736 | tf_op jit(solution)/shard_map/while/body/eval_jaxpr/ppermute | solution.py:23
  654.0 26.4 %collective-permute-start.15 = (f32[3,1,2048]{2,1,0:T(1,128)}, f32[3,1,2048]{2,1,0:T(1,128)S(1)}, u32[]{:S(2)}, u32[]{:S(2)}) collective-permute-start(f32[3,1,2048]{2,1,0:T(1,128)} %get-tuple-element.1095), channel_id=1, source_target_pairs={{0,2},{2,4},{4,6},{6,8},{8,10},{10,12},{12,14},{1,3},{3,5},{5,7},{... | collective-permute-start | bytes 73736 | tf_op jit(solution)/shard_map/while/body/eval_jaxpr/ppermute | solution.py:21
  671.4 24.0 %collective-permute-start.22 = (f32[3,1,2048]{2,1,0:T(1,128)S(1)}, f32[3,1,2048]{2,1,0:T(1,128)S(1)}, u32[]{:S(2)}, u32[]{:S(2)}) collective-permute-start(f32[3,1,2048]{2,1,0:T(1,128)S(1)} %get-tuple-element.1151), channel_id=1, source_target_pairs={{2,0},{4,2},{6,4},{8,6},{10,8},{12,10},{14,12},{3,1},{5,3},{7,5},{... | collective-permute-start | bytes 73736 | tf_op jit(solution)/shard_map/while/body/eval_jaxpr/ppermute | solution.py:23
  672.7 22.7 %collective-permute-start.23 = (f32[3,1,2048]{2,1,0:T(1,128)S(1)}, f32[3,1,2048]{2,1,0:T(1,128)S(1)}, u32[]{:S(2)}, u32[]{:S(2)}) collective-permute-start(f32[3,1,2048]{2,1,0:T(1,128)S(1)} %get-tuple-element.1152), channel_id=1, source_target_pairs={{0,2},{2,4},{4,6},{6,8},{8,10},{10,12},{12,14},{1,3},{3,5},{5,7},{... | collective-permute-start | bytes 73736 | tf_op jit(solution)/shard_map/while/body/eval_jaxpr/ppermute | solution.py:21
  718.2 18.9 %collective-permute-start.8 = (f32[3,1,2048]{2,1,0:T(1,128)S(1)}, f32[3,1,2048]{2,1,0:T(1,128)S(1)}, u32[]{:S(2)}, u32[]{:S(2)}) collective-permute-start(f32[3,1,2048]{2,1,0:T(1,128)S(1)} %get-tuple-element.1032), channel_id=1, source_target_pairs={{2,0},{4,2},{6,4},{8,6},{10,8},{12,10},{14,12},{3,1},{5,3},{7,5},{... | collective-permute-start | bytes 73736 | tf_op jit(solution)/shard_map/while/body/eval_jaxpr/ppermute | solution.py:23
  719.5 17.6 %collective-permute-start.9 = (f32[3,1,2048]{2,1,0:T(1,128)S(1)}, f32[3,1,2048]{2,1,0:T(1,128)S(1)}, u32[]{:S(2)}, u32[]{:S(2)}) collective-permute-start(f32[3,1,2048]{2,1,0:T(1,128)S(1)} %get-tuple-element.1033), channel_id=1, source_target_pairs={{0,2},{2,4},{4,6},{6,8},{8,10},{10,12},{12,14},{1,3},{3,5},{5,7},{... | collective-permute-start | bytes 73736 | tf_op jit(solution)/shard_map/while/body/eval_jaxpr/ppermute | solution.py:21
  725.9 28.4 %collective-permute-start.16 = (f32[3,1,2048]{2,1,0:T(1,128)S(1)}, f32[3,1,2048]{2,1,0:T(1,128)S(1)}, u32[]{:S(2)}, u32[]{:S(2)}) collective-permute-start(f32[3,1,2048]{2,1,0:T(1,128)S(1)} %get-tuple-element.1112), channel_id=1, source_target_pairs={{2,0},{4,2},{6,4},{8,6},{10,8},{12,10},{14,12},{3,1},{5,3},{7,5},{... | collective-permute-start | bytes 73736 | tf_op jit(solution)/shard_map/while/body/eval_jaxpr/ppermute | solution.py:23
  727.2 27.1 %collective-permute-start.17 = (f32[3,1,2048]{2,1,0:T(1,128)S(1)}, f32[3,1,2048]{2,1,0:T(1,128)S(1)}, u32[]{:S(2)}, u32[]{:S(2)}) collective-permute-start(f32[3,1,2048]{2,1,0:T(1,128)S(1)} %get-tuple-element.1113), channel_id=1, source_target_pairs={{0,2},{2,4},{4,6},{6,8},{8,10},{10,12},{12,14},{1,3},{3,5},{5,7},{... | collective-permute-start | bytes 73736 | tf_op jit(solution)/shard_map/while/body/eval_jaxpr/ppermute | solution.py:21
  747.4 23.9 %collective-permute-start.10 = (f32[3,1,2048]{2,1,0:T(1,128)S(1)}, f32[3,1,2048]{2,1,0:T(1,128)S(1)}, u32[]{:S(2)}, u32[]{:S(2)}) collective-permute-start(f32[3,1,2048]{2,1,0:T(1,128)S(1)} %get-tuple-element.1058), channel_id=1, source_target_pairs={{2,0},{4,2},{6,4},{8,6},{10,8},{12,10},{14,12},{3,1},{5,3},{7,5},{... | collective-permute-start | bytes 73736 | tf_op jit(solution)/shard_map/while/body/eval_jaxpr/ppermute | solution.py:23
  748.7 22.6 %collective-permute-start.11 = (f32[3,1,2048]{2,1,0:T(1,128)S(1)}, f32[3,1,2048]{2,1,0:T(1,128)S(1)}, u32[]{:S(2)}, u32[]{:S(2)}) collective-permute-start(f32[3,1,2048]{2,1,0:T(1,128)S(1)} %get-tuple-element.1059), channel_id=1, source_target_pairs={{0,2},{2,4},{4,6},{6,8},{8,10},{10,12},{12,14},{1,3},{3,5},{5,7},{... | collective-permute-start | bytes 73736 | tf_op jit(solution)/shard_map/while/body/eval_jaxpr/ppermute | solution.py:21
  764.1 19.5 %collective-permute-start.18 = (f32[3,1,2048]{2,1,0:T(1,128)S(1)}, f32[3,1,2048]{2,1,0:T(1,128)S(1)}, u32[]{:S(2)}, u32[]{:S(2)}) collective-permute-start(f32[3,1,2048]{2,1,0:T(1,128)S(1)} %get-tuple-element.1125), channel_id=1, source_target_pairs={{2,0},{4,2},{6,4},{8,6},{10,8},{12,10},{14,12},{3,1},{5,3},{7,5},{... | collective-permute-start | bytes 73736 | tf_op jit(solution)/shard_map/while/body/eval_jaxpr/ppermute | solution.py:23
  765.4 18.2 %collective-permute-start.19 = (f32[3,1,2048]{2,1,0:T(1,128)S(1)}, f32[3,1,2048]{2,1,0:T(1,128)S(1)}, u32[]{:S(2)}, u32[]{:S(2)}) collective-permute-start(f32[3,1,2048]{2,1,0:T(1,128)S(1)} %get-tuple-element.1126), channel_id=1, source_target_pairs={{0,2},{2,4},{4,6},{6,8},{8,10},{10,12},{12,14},{1,3},{3,5},{5,7},{... | collective-permute-start | bytes 73736 | tf_op jit(solution)/shard_map/while/body/eval_jaxpr/ppermute | solution.py:21
  805.6 17.7 %collective-permute-start.12 = (f32[3,1,2048]{2,1,0:T(1,128)}, f32[3,1,2048]{2,1,0:T(1,128)S(1)}, u32[]{:S(2)}, u32[]{:S(2)}) collective-permute-start(f32[3,1,2048]{2,1,0:T(1,128)} %get-tuple-element.1076), channel_id=1, source_target_pairs={{2,0},{4,2},{6,4},{8,6},{10,8},{12,10},{14,12},{3,1},{5,3},{7,5},{... | collective-permute-start | bytes 73736 | tf_op jit(solution)/shard_map/while/body/eval_jaxpr/ppermute | solution.py:23
  806.9 16.4 %collective-permute-start.13 = (f32[3,1,2048]{2,1,0:T(1,128)S(1)}, f32[3,1,2048]{2,1,0:T(1,128)S(1)}, u32[]{:S(2)}, u32[]{:S(2)}) collective-permute-start(f32[3,1,2048]{2,1,0:T(1,128)S(1)} %get-tuple-element.1077), channel_id=1, source_target_pairs={{0,2},{2,4},{4,6},{6,8},{8,10},{10,12},{12,14},{1,3},{3,5},{5,7},{... | collective-permute-start | bytes 73736 | tf_op jit(solution)/shard_map/while/body/eval_jaxpr/ppermute | solution.py:21
  815.1 35.7 %collective-permute-start.20 = (f32[3,1,2048]{2,1,0:T(1,128)S(1)}, f32[3,1,2048]{2,1,0:T(1,128)S(1)}, u32[]{:S(2)}, u32[]{:S(2)}) collective-permute-start(f32[3,1,2048]{2,1,0:T(1,128)S(1)} %get-tuple-element.1138), channel_id=1, source_target_pairs={{2,0},{4,2},{6,4},{8,6},{10,8},{12,10},{14,12},{3,1},{5,3},{7,5},{... | collective-permute-start | bytes 73736 | tf_op jit(solution)/shard_map/while/body/eval_jaxpr/ppermute | solution.py:23
  816.4 34.4 %collective-permute-start.21 = (f32[3,1,2048]{2,1,0:T(1,128)S(1)}, f32[3,1,2048]{2,1,0:T(1,128)S(1)}, u32[]{:S(2)}, u32[]{:S(2)}) collective-permute-start(f32[3,1,2048]{2,1,0:T(1,128)S(1)} %get-tuple-element.1139), channel_id=1, source_target_pairs={{0,2},{2,4},{4,6},{6,8},{8,10},{10,12},{12,14},{1,3},{3,5},{5,7},{... | collective-permute-start | bytes 73736 | tf_op jit(solution)/shard_map/while/body/eval_jaxpr/ppermute | solution.py:21
  871.6 27.9 %collective-permute-start.14 = (f32[3,1,2048]{2,1,0:T(1,128)}, f32[3,1,2048]{2,1,0:T(1,128)S(1)}, u32[]{:S(2)}, u32[]{:S(2)}) collective-permute-start(f32[3,1,2048]{2,1,0:T(1,128)} %get-tuple-element.1094), channel_id=1, source_target_pairs={{2,0},{4,2},{6,4},{8,6},{10,8},{12,10},{14,12},{3,1},{5,3},{7,5},{... | collective-permute-start | bytes 73736 | tf_op jit(solution)/shard_map/while/body/eval_jaxpr/ppermute | solution.py:23
  872.9 26.6 %collective-permute-start.15 = (f32[3,1,2048]{2,1,0:T(1,128)}, f32[3,1,2048]{2,1,0:T(1,128)S(1)}, u32[]{:S(2)}, u32[]{:S(2)}) collective-permute-start(f32[3,1,2048]{2,1,0:T(1,128)} %get-tuple-element.1095), channel_id=1, source_target_pairs={{0,2},{2,4},{4,6},{6,8},{8,10},{10,12},{12,14},{1,3},{3,5},{5,7},{... | collective-permute-start | bytes 73736 | tf_op jit(solution)/shard_map/while/body/eval_jaxpr/ppermute | solution.py:21
  890.2 24.2 %collective-permute-start.22 = (f32[3,1,2048]{2,1,0:T(1,128)S(1)}, f32[3,1,2048]{2,1,0:T(1,128)S(1)}, u32[]{:S(2)}, u32[]{:S(2)}) collective-permute-start(f32[3,1,2048]{2,1,0:T(1,128)S(1)} %get-tuple-element.1151), channel_id=1, source_target_pairs={{2,0},{4,2},{6,4},{8,6},{10,8},{12,10},{14,12},{3,1},{5,3},{7,5},{... | collective-permute-start | bytes 73736 | tf_op jit(solution)/shard_map/while/body/eval_jaxpr/ppermute | solution.py:23
  891.5 22.9 %collective-permute-start.23 = (f32[3,1,2048]{2,1,0:T(1,128)S(1)}, f32[3,1,2048]{2,1,0:T(1,128)S(1)}, u32[]{:S(2)}, u32[]{:S(2)}) collective-permute-start(f32[3,1,2048]{2,1,0:T(1,128)S(1)} %get-tuple-element.1152), channel_id=1, source_target_pairs={{0,2},{2,4},{4,6},{6,8},{8,10},{10,12},{12,14},{1,3},{3,5},{5,7},{... | collective-permute-start | bytes 73736 | tf_op jit(solution)/shard_map/while/body/eval_jaxpr/ppermute | solution.py:21
  947.3 32.4 %collective-permute-start.28 = (f32[3,8,2048]{2,0,1:T(4,128)S(1)}, f32[3,8,2048]{2,0,1:T(4,128)S(1)}, u32[]{:S(2)}, u32[]{:S(2)}) collective-permute-start(f32[3,8,2048]{2,0,1:T(4,128)S(1)} %get-tuple-element.467), channel_id=1, source_target_pairs={{1,0},{3,2},{5,4},{7,6},{9,8},{11,10},{13,12},{15,14},{17,16},{19,... | collective-permute-start | bytes 589832 | tf_op jit(solution)/shard_map/ppermute | solution.py:33
  980.0 6.5 collective-permute-start.30
  (186 other events, 442.8 us)
where the time goes:
time: 1010 us; the launch traced here: 999 us
  matrix products  408 us (40%)
  starting transfers between devices  248 us (25%)
  local copies, waits for them, and re-layouts  126 us (12%)
  other arithmetic  85.6 us (8%)
  loops' own time  63.6 us (6%)
  waiting for transfers between devices  35.4 us (4%)
  blocking collectives  31.1 us (3%)
    dot_general x315, matrix products, advance(): jnp.einsum('oc,cij->oij', weights[stencil_index], offset_view(widened, of...  228 us
    ppermute x39, starting transfers between devices, with_halo(): lax.ppermute(tail, axis, [(i, (i + 1) % count) for i in range(ends)])  196 us
    dot_general x108, matrix products, closure_terms(): terms.append(jnp.einsum('oij,cij->oc', adjoint, shifted, precision=highest))  179 us
    ppermute x39, starting transfers between devices, with_halo(): lax.ppermute(head, axis, [((i + 1) % count, i) for i in range(ends)])  50.3 us
    while x282, local copies, waits for them, and re-layouts  36.9 us
    ppermute x39, waiting for transfers between devices, with_halo(): lax.ppermute(head, axis, [((i + 1) % count, i) for i in range(ends)])  34.3 us
    another operation x1, loops' own time, body(): _, saved_blocks = lax.scan(first_pass, checkpoints[0], block_numbers)  32.6 us
    psum x1, blocking collectives, body(): gradient_sum = lax.psum(gradient, ('space', 'cuts'))  31.1 us
  transfers between devices with their start and end apart: 79, of which 10 were waited for; matrix products, arithmetic and copies ran while one was open for 27% of the time, Pallas kernels for 0%

commit v1 on v0

v1 whole, which is shorter than its diff:
```python
import functools

import jax
import jax.numpy as jnp
from jax import lax
from jax.experimental import pallas as pl
from jax.experimental.pallas import tpu as pltpu
from jax.sharding import PartitionSpec as P

FINE = 12
fine_rate = 0.05
LANES = 128
HALF = LANES // 2
MESH = pl.DeviceIdType.MESH
BLOCK = 2
GRAD_BLOCK = 2


def kernel(
    geo,
    depth_ref, table_ref, counts_ref, weights_ref, state_ref, adjoint_ref,
    out_ref, grad_ref,
    send_adj, send_state, recv_adj, recv_state, depth_half, depth_east, depth_west, friction,
    states, adjoints, ending, new_start, back, landed, products, grad_parts, side, coefs,
    adj_send, adj_recv, state_send, state_recv, cross_send, cross_recv,
    back_send, back_recv, grad_send, grad_recv,
):
    n, slices, strip, rows, cols, width, share = geo
    own_tiles = width // LANES
    tiles = own_tiles + 1
    span = tiles * LANES
    lead = rows // 8
    workers = n // share
    me = lax.axis_index("space")
    cut = lax.axis_index("cuts")
    my_worker = me // share
    last = cut == slices - 1

    barrier = pltpu.get_barrier_semaphore()
    partners = [(a, b) for b in range(slices) for a in range(n) if (a, b) != (0, 0)]
    for a, b in partners:
        pl.semaphore_signal(
            barrier, inc=1,
            device_id={"space": lax.rem(me + a, n), "cuts": lax.rem(cut + b, slices)},
            device_id_type=MESH,
        )

    lane = lax.broadcasted_iota(jnp.int32, (8, LANES), 1)
    sub = lax.broadcasted_iota(jnp.int32, (8, LANES), 0)

    def fields_of(ref, start):
        return ref[:, :, pl.ds(pl.multiple_of(start, LANES), LANES)]

    def pack(target, ref, worker, with_depth):
        first = worker * width
        after = jnp.minimum(first + width, cols - LANES)
        before = jnp.maximum(first - LANES, 0)
        right_in = worker < workers - 1
        left_in = worker > 0
        low = lane < HALF
        for t in range(own_tiles):
            target[pl.ds(0, 3), t] = fields_of(ref, first + t * LANES)
        right = jnp.where(right_in, fields_of(ref, after), 0.0)
        left = jnp.where(left_in, fields_of(ref, before), 0.0)
        target[pl.ds(0, 3), own_tiles] = jnp.where(low, right, left)
        if with_depth:
            def depth_at(start):
                at = pl.ds(pl.multiple_of(start, LANES), LANES)
                return depth_ref[:, at].astype(jnp.float32)

            for t in range(own_tiles):
                target[3, t] = depth_at(first + t * LANES)
            target[3, own_tiles] = jnp.where(low, depth_at(after), depth_at(before))

    my_rows = pl.ds(pl.multiple_of(me * strip, strip), strip)

    def outward(buffer, landing, sends, receives, k):
        return pltpu.make_async_remote_copy(
            src_ref=buffer.at[k],
            dst_ref=landing.at[:, :, my_rows, :],
            send_sem=sends.at[k],
            recv_sem=receives.at[k],
            device_id={"space": lax.rem(me + k, n)},
            device_id_type=MESH,
        )

    for k in range(1, n):
        pack(send_adj.at[k], adjoint_ref, lax.rem(me + k, n) // share, True)
    pl.semaphore_wait(barrier, len(partners))
    for k in range(1, n):
        outward(send_adj, recv_adj, adj_send, adj_recv, k).start()
    for k in range(1, n):
        pack(send_state.at[k], state_ref, lax.rem(me + k, n) // share, False)
        outward(send_state, recv_state, state_send, state_recv, k).start()
    pack(recv_adj.at[:, :, my_rows, :], adjoint_ref, my_worker, True)
    pack(recv_state.at[:, :, my_rows, :], state_ref, my_worker, False)

    total = jnp.where(last, counts_ref[slices - 1], counts_ref[0])
    for s in range(1, slices - 1):
        total = jnp.where(cut == s, counts_ref[s], total)
    coarse_rate = total.astype(jnp.float32) * fine_rate

    def fold(k, o, c, sign):
        if k == 4:
            return 0.0
        if o == 0 and c != 0 or c == 0 and o != 0:
            field = o + c
            side_of = {5: (1, 1), 3: (1, -1), 7: (2, 1), 1: (2, -1)}.get(k)
            if side_of is not None and side_of[0] == field:
                if (sign < 0) == (c == 0):
                    return sign * side_of[1] * 0.5
        return 0.0

    for k in range(9):
        for o in range(3):
            for c in range(3):
                at = (k * 3 + o) * 3 + c
                one = 1.0 if k == 4 and o == c else 0.0
                forward = weights_ref[k, o, c] + fold(k, o, c, -1.0)
                backward = weights_ref[8 - k, c, o] + fold(k, o, c, 1.0)
                coefs[0, at] = one + fine_rate * forward
                coefs[1, at] = one + fine_rate * backward
                coefs[2, at] = one + coarse_rate * backward

    lane_wide = lax.broadcasted_iota(jnp.int32, (8, span), 1) - width
    in_left = (lane_wide >= HALF) & (my_worker == 0)
    in_right = (lane_wide >= 0) & (lane_wide < HALF) & (my_worker == workers - 1)
    inside = jnp.where(in_left | in_right, 0.0, 1.0)
    side[...] = inside

    sub_wide = lax.broadcasted_iota(jnp.int32, (8, span), 0)

    def wrap(ref):
        for c in range(ref.shape[0]):
            ref[c, 0] = jnp.where(sub_wide == 0, 0.0, pltpu.roll(ref[c, lead], 1, 0))
            ref[c, lead + 1] = jnp.where(sub_wide == 7, 0.0, pltpu.roll(ref[c, 1], 7, 0))

    def arrive(landing, field, i):
        return [landing[field, t, pl.ds(i, 8, stride=lead), :] for t in range(tiles)]

    def spread(landing, target):
        def row(i, carry):
            for c in range(3):
                for t, tile in enumerate(arrive(landing, c, i)):
                    target[c, i + 1, :, t * LANES:(t + 1) * LANES] = tile
            return carry

        lax.fori_loop(0, lead, row, 0)
        wrap(target)

    for k in range(1, n):
        outward(send_adj, recv_adj, adj_send, adj_recv, k).wait_recv()
    spread(recv_adj, adjoints.at[FINE])

    def coefficient_row(i, carry):
        for t, kind in enumerate(arrive(recv_adj, 3, i)):
            depth = jnp.full((8, LANES), table_ref[0, 0], jnp.float32)
            drag = jnp.full((8, LANES), table_ref[1, 0], jnp.float32)
            for j in range(1, table_ref.shape[1]):
                same = kind == float(j)
                depth = jnp.where(same, table_ref[0, j], depth)
                drag = jnp.where(same, table_ref[1, j], drag)
            depth_half[0, i + 1, :, t * LANES:(t + 1) * LANES] = 0.5 * depth
            friction[i, :, t * LANES:(t + 1) * LANES] = drag
        return carry

    lax.fori_loop(0, lead, coefficient_row, 0)
    wrap(depth_half)

    def shift_row(i, carry):
        here = depth_half[0, i + 1]
        depth_east[i] = pltpu.roll(here, span - 1, 1)
        depth_west[i] = pltpu.roll(here, 1, 1)
        return carry

    lax.fori_loop(0, lead, shift_row, 0)

    def stencil(load, which, rate, transposed, i):
        acc = [None, None, None]
        rim = {}
        for c in range(3):
            x = load(c, pl.ds(i, BLOCK + 2))
            moved = (pltpu.roll(x, 1, 2), x, pltpu.roll(x, span - 1, 2))
            for dc in range(3):
                for dr in range(3):
                    view = moved[dc][dr:dr + BLOCK]
                    rim[c, dr, dc] = view
                    for o in range(3):
                        term = coefs[which, ((3 * dr + dc) * 3 + o) * 3 + c] * view
                        acc[o] = term if acc[o] is None else acc[o] + term
            drag = rate * friction[pl.ds(i, BLOCK)]
            if c:
                acc[c] = acc[c] - drag * rim[c, 1, 1]
            if transposed and c == 0:
                here = pl.ds(i, BLOCK)
                acc[1] = acc[1] + rate * (
                    depth_east[here] * rim[0, 1, 2] - depth_west[here] * rim[0, 1, 0]
                )
                acc[2] = acc[2] + rate * (
                    depth_half[0, pl.ds(i + 2, BLOCK)] * rim[0, 2, 1]
                    - depth_half[0, pl.ds(i, BLOCK)] * rim[0, 0, 1]
                )
        if not transposed:
            slope = (rim[1, 1, 2] - rim[1, 1, 0]) + (rim[2, 2, 1] - rim[2, 0, 1])
            acc[0] = acc[0] - rate * (depth_half[0, pl.ds(i + 1, BLOCK)] * slope)
        return [a * side[...] for a in acc]

    blocks = lead // BLOCK

    def adjoint_step(turn, carry):
        step = FINE - 1 - turn
        active = step < total

        def one(b, inner):
            i = b * BLOCK
            found = stencil(lambda c, at: adjoints[step + 1, c, at], 1, fine_rate, True, i)
            for c in range(3):
                old = adjoints[step + 1, c, pl.ds(i + 1, BLOCK)]
                adjoints[step, c, pl.ds(i + 1, BLOCK)] = jnp.where(active, found[c], old)
            return inner

        lax.fori_loop(0, blocks, one, 0)
        wrap(adjoints.at[step])
        return carry

    lax.fori_loop(0, FINE, adjoint_step, 0)

    def homeward(k):
        target = lax.rem(me + k, n)
        return pltpu.make_async_remote_copy(
            src_ref=back.at[:, :, pl.ds(pl.multiple_of(target * strip, strip), strip), :],
            dst_ref=landed.at[:, pl.ds(my_worker * own_tiles, own_tiles), :, :],
            send_sem=back_send.at[k],
            recv_sem=back_recv.at[k],
            device_id={"space": target},
            device_id_type=MESH,
        )

    def leads(device):
        return lax.rem(device, share) == 0

    def when(condition):
        return pl.when(condition) if share > 1 else (lambda f: f())

    def correct():
        for c in range(3):
            def change(i, carry):
                ending[c, i] = ending[c, i] - adjoints[FINE, c, i]
                return carry

            lax.fori_loop(0, lead + 2, change, 0)

        def one(b, carry):
            i = b * BLOCK
            found = stencil(lambda c, at: ending[c, at], 2, coarse_rate, True, i)
            for c in range(3):
                new_start[c, pl.ds(i + 1, BLOCK)] = (
                    found[c] + adjoints[0, c, pl.ds(i + 1, BLOCK)]
                )
            return carry

        lax.fori_loop(0, blocks, one, 0)
        wrap(new_start)

    def go_home():
        def row(i, carry):
            for c in range(3):
                for t in range(own_tiles):
                    back[c, t, pl.ds(i, 8, stride=lead), :] = new_start[
                        c, i + 1, :, t * LANES:(t + 1) * LANES
                    ]
            return carry

        lax.fori_loop(0, lead, row, 0)

        @when(leads(me))
        def _():
            for k in range(1, n):
                homeward(k).start()
            landed[:, pl.ds(my_worker * own_tiles, own_tiles)] = back[:, :, my_rows, :]

    def across():
        return pltpu.make_async_remote_copy(
            src_ref=new_start,
            dst_ref=ending,
            send_sem=cross_send,
            recv_sem=cross_recv,
            device_id={"cuts": lax.rem(cut + slices - 1, slices)},
            device_id_type=MESH,
        )

    @pl.when(last)
    def _():
        for c in range(3):
            def change(i, carry):
                ending[c, i] = adjoints[FINE, c, i]
                return carry

            lax.fori_loop(0, lead + 2, change, 0)
        correct()
        if slices > 1:
            across().start()
        go_home()

    for k in range(1, n):
        outward(send_state, recv_state, state_send, state_recv, k).wait_recv()
    spread(recv_state, states.at[0])

    def forward_step(step, carry):
        def one(b, inner):
            i = b * BLOCK
            found = stencil(lambda c, at: states[step, c, at], 0, fine_rate, False, i)
            for c in range(3):
                states[step + 1, c, pl.ds(i + 1, BLOCK)] = found[c]
            return inner

        lax.fori_loop(0, blocks, one, 0)
        wrap(states.at[step + 1])
        return carry

    lax.fori_loop(0, FINE - 1, forward_step, 0)

    if slices > 1:
        @pl.when(jnp.logical_not(last))
        def _():
            across().wait_recv()
            correct()
            go_home()

            @pl.when(cut > 0)
            def _():
                across().start()

    grad_scale = fine_rate * float(rows * cols * slices) ** (-0.5) / share
    zero = jnp.zeros((8, LANES), jnp.float32)
    own = own_tiles * LANES

    for c in range(3):
        def pairs(turn, sums):
            step = turn // (lead // GRAD_BLOCK)
            i = (turn % (lead // GRAD_BLOCK)) * GRAD_BLOCK
            factor = jnp.where(step < total, grad_scale, 0.0)
            x = states[step, c, pl.ds(i, GRAD_BLOCK + 2)]
            lam = [
                factor * adjoints[step + 1, o, pl.ds(i + 1, GRAD_BLOCK), :, 0:own]
                for o in range(3)
            ]
            moved = (pltpu.roll(x, 1, 2), x, pltpu.roll(x, span - 1, 2))
            result = []
            for dr in range(3):
                for dc in range(3):
                    view = moved[dc][dr:dr + GRAD_BLOCK, :, 0:own]
                    for o in range(3):
                        prod = view * lam[o]
                        part = sums[len(result)]
                        for r in range(GRAD_BLOCK):
                            for t in range(own_tiles):
                                part = part + prod[r, :, t * LANES:(t + 1) * LANES]
                        result.append(part)
            return tuple(result)

        sums = lax.fori_loop(0, FINE * (lead // GRAD_BLOCK), pairs, (zero,) * 27)
        for at in range(27):
            products[at * 3 + c] = sums[at]
    for at in range(81, products.shape[0]):
        products[at] = zero

    column = jnp.sum(jnp.sum(products[...], axis=1), axis=1, keepdims=True)
    count = products.shape[0]
    diagonal = lax.broadcasted_iota(jnp.int32, (count, LANES), 0) == lax.broadcasted_iota(
        jnp.int32, (count, LANES), 1
    )
    line = jnp.sum(jnp.where(diagonal, column, 0.0), axis=0, keepdims=True)
    grad_parts[0] = jnp.broadcast_to(line, (8, LANES))

    def share_grad(j):
        a, b = partners[j]
        return pltpu.make_async_remote_copy(
            src_ref=grad_parts.at[0],
            dst_ref=grad_parts.at[j + 1],
            send_sem=grad_send.at[j],
            recv_sem=grad_recv.at[j],
            device_id={"space": lax.rem(me + a, n), "cuts": lax.rem(cut + b, slices)},
            device_id_type=MESH,
        )

    for j in range(len(partners)):
        share_grad(j).start()

    for k in range(1, n):
        @when(leads(lax.rem(me + n - k, n)))
        def _():
            homeward(k).wait_recv()

    for t in range(cols // LANES):
        out_ref[0, :, :, t * LANES:(t + 1) * LANES] = landed[:, t]

    whole = grad_parts[0]
    for j in range(len(partners)):
        share_grad(j).wait_recv()
        whole = whole + grad_parts[j + 1]
    grad_ref[...] = whole

    for k in range(1, n):
        outward(send_adj, recv_adj, adj_send, adj_recv, k).wait_send()
        outward(send_state, recv_state, state_send, state_recv, k).wait_send()

    @when(leads(me))
    def _():
        for k in range(1, n):
            homeward(k).wait_send()

    if slices > 1:
        @pl.when(cut > 0)
        def _():
            across().wait_send()

    for j in range(len(partners)):
        share_grad(j).wait_send()


def body(depth_class, coef_table, step_counts, closure_weights, checkpoints, old_adjoint):
    n = lax.axis_size("space")
    slices = lax.axis_size("cuts")
    strip, cols = depth_class.shape
    rows = strip * n
    width = max(cols // n, LANES)
    share = width * n // cols
    tiles = width // LANES + 1
    span = tiles * LANES
    lead = rows // 8
    geo = (n, slices, strip, rows, cols, width, share)
    partners = n * slices - 1
    f32 = jnp.float32
    vmem = pl.BlockSpec(memory_space=pltpu.VMEM)
    smem = pl.BlockSpec(memory_space=pltpu.SMEM)
    dma = pltpu.SemaphoreType.DMA
    new_adjoint, grad = pl.pallas_call(
        functools.partial(kernel, geo),
        out_shape=(
            jax.ShapeDtypeStruct((1, 3, strip, cols), f32),
            jax.ShapeDtypeStruct((8, LANES), f32),
        ),
        in_specs=[vmem, smem, smem, smem, vmem, vmem],
        out_specs=(vmem, vmem),
        scratch_shapes=[
            pltpu.VMEM((n, 4, tiles, strip, LANES), f32),
            pltpu.VMEM((n, 3, tiles, strip, LANES), f32),
            pltpu.VMEM((4, tiles, rows, LANES), f32),
            pltpu.VMEM((3, tiles, rows, LANES), f32),
            pltpu.VMEM((1, lead + 2, 8, span), f32),
            pltpu.VMEM((lead, 8, span), f32),
            pltpu.VMEM((lead, 8, span), f32),
            pltpu.VMEM((lead, 8, span), f32),
            pltpu.VMEM((FINE, 3, lead + 2, 8, span), f32),
            pltpu.VMEM((FINE + 1, 3, lead + 2, 8, span), f32),
            pltpu.VMEM((3, lead + 2, 8, span), f32),
            pltpu.VMEM((3, lead + 2, 8, span), f32),
            pltpu.VMEM((3, tiles - 1, rows, LANES), f32),
            pltpu.VMEM((3, cols // LANES, strip, LANES), f32),
            pltpu.VMEM((88, 8, LANES), f32),
            pltpu.VMEM((partners + 1, 8, LANES), f32),
            pltpu.VMEM((8, span), f32),
            pltpu.SMEM((3, 81), f32),
            dma((n,)), dma((n,)), dma((n,)), dma((n,)),
            dma(()), dma(()),
            dma((n,)), dma((n,)),
            dma((partners,)), dma((partners,)),
        ],
        compiler_params=pltpu.CompilerParams(
            collective_id=0, has_side_effects=True, vmem_limit_bytes=48 * 1024 * 1024
        ),
    )(depth_class, coef_table, step_counts, closure_weights, checkpoints[0], old_adjoint[0])
    return new_adjoint, grad[0, :81].reshape(9, 3, 3)


def solution(mesh):
    return jax.shard_map(
        body,
        mesh=mesh,
        in_specs=(
            P("space", None),
            P(),
            P(),
            P("member", None, None),
            P(("member", "cuts"), None, "space", None),
            P(("member", "cuts"), None, "space", None),
        ),
        out_specs=(P(("member", "cuts"), None, "space", None), P("member", None, None)),
        check_vma=False,
    )
```

time: 1010 us -> 68.4 us (0.07); the launches traced: 999 us -> 68.2 us
  matrix products: 408 us -> 0 us
  starting transfers between devices: 248 us -> 0 us
  local copies, waits for them, and re-layouts: 126 us -> 5 us
  other arithmetic: 85.6 us -> 0 us
  loops' own time: 63.6 us -> 0 us
  Pallas kernels: 0 us -> 62.5 us
  waiting for transfers between devices: 35.4 us -> 0 us
  blocking collectives: 31.1 us -> 0 us
    dot_general x424 -> x0, matrix products: 408 us -> none  [the longest x315 228 us: advance(): jnp.einsum('oc,cij->oij', weights[stencil_index], offset_view(widened, of...]
    ppermute x79 -> x0, starting transfers between devices: 248 us -> none  [the longest x39 196 us: with_halo(): lax.ppermute(tail, axis, [(i, (i + 1) % count) for i in range(ends)])]
    another operation x2 -> x0, loops' own time: 63.6 us -> none  [the longest x1 32.6 us: body(): _, saved_blocks = lax.scan(first_pass, checkpoints[0], block_numbers)]
    pallas_call x0 -> x1, Pallas kernels: none -> 62.5 us  [body(): pl.pallas_call(functools.partial(kernel, geo), out_shape=(jax.ShapeDtypeS...]
    while x283 -> x0, local copies, waits for them, and re-layouts: 36.9 us -> none
    ppermute x79 -> x0, waiting for transfers between devices: 35.4 us -> none  [the longest x39 34.3 us: with_halo(): lax.ppermute(head, axis, [((i + 1) % count, i) for i in range(ends)])]
    psum x1 -> x0, blocking collectives: 31.1 us -> none  [body(): gradient_sum = lax.psum(gradient, ('space', 'cuts'))]
    select_n x34 -> x0, other arithmetic: 29.3 us -> none  [the longest x21 25.7 us: forward_block(): state_now = jnp.where(active, stepped, state_now)]
  transfers between devices with their start and end apart: 79 -> 0, of which waited for: 10 -> 0; matrix products, arithmetic and copies ran while one was open for 27% -> 0% of each run, Pallas kernels for 0% -> 0%
where the time goes in v1:
time: 68.4 us; the launch traced here: 68.2 us
  Pallas kernels  62.5 us (91%)
  local copies, waits for them, and re-layouts  5 us (7%)
    pallas_call x1, Pallas kernels, body(): pl.pallas_call(functools.partial(kernel, geo), out_shape=(jax.ShapeDtypeS...  62.5 us
    unnamed x13, local copies, waits for them, and re-layouts  4.88 us

profile of v1, /device:TPU:0, one launch (start us, length us, event | category | flops | bytes accessed | tf_op | source)
XLA Modules:
  0.0 68.2 jit_solution(6428102037621137127)
XLA Ops:
  0.6 0.0 copy-start.3
  0.6 0.0 copy-start.4
  0.7 0.8 %copy.10.weights_ref = f32[9,3,3]{2,1,0:T(4,128)S(1)} copy(f32[9,3,3]{0,2,1:T(4,128)} %param.9) | data formatting | bytes 648 | tf_op args[3]
  1.5 0.0 copy-done.3
  1.5 0.0 copy-done.4
  1.5 0.0 copy-start
  1.5 0.9 %copy-done = f32[1,3,8,2048]{3,2,1,0:T(8,128)S(1)} copy-done((f32[1,3,8,2048]{3,2,1,0:T(8,128)S(1)}, f32[1,3,8,2048]{3,2,1,0:T(8,128)}, u32[]{:S(2)}) %copy-start) | copy-done | bytes 196632
  2.4 0.0 copy-start.1
  2.4 0.9 %copy-done.1 = f32[1,3,8,2048]{3,2,1,0:T(8,128)S(1)} copy-done((f32[1,3,8,2048]{3,2,1,0:T(8,128)S(1)}, f32[1,3,8,2048]{3,2,1,0:T(8,128)}, u32[]{:S(2)}) %copy-start.1) | copy-done | bytes 196632
  3.3 0.0 copy-start.2
  3.3 0.8 %copy-done.2 = s32[8,2048]{1,0:T(8,128)S(1)} copy-done((s32[8,2048]{1,0:T(8,128)S(1)}, s32[8,2048]{1,0:T(8,128)}, u32[]{:S(2)}) %copy-start.2) | copy-done | bytes 65560
  4.2 62.5 %shard_map.77 = (f32[1,3,8,2048]{3,2,1,0:T(8,128)S(1)}, f32[8,128]{1,0:T(8,128)S(1)}) custom-call(s32[8,2048]{1,0:T(8,128)S(1)} %copy-done.2, f32[2,8]{1,0:T(2,128)S(1)} %copy-done.3, s32[2]{0:T(128)S(1)} %copy-done.4, f32[9,3,3]{2,1,0:T(4,128)S(1)} %copy.10.weights_ref, f32[3,8,2048]{2,1,0:T(8,128)S(1)} %bitcast.2, f32[3,8,2048]{2,1,0:T(8,128)S(1)} %bitcast.3), custom_call_target="tpu_custom_call" | custom-call | tf_op jit(solution)/shard_map/pallas_call | solution.py:438
  66.7 0.1 reshape_squeeze.3
  66.8 0.7 %copy.11 = f32[9,3,3]{0,2,1:T(4,128)} copy(f32[9,3,3]{2,1,0:T(4,128)S(1)} %reshape_squeeze.3) | data formatting | bytes 648
  67.5 0.7 copy.13
  (1 shorter events, 0.0 us)
Async XLA Ops:
  0.6 0.8 %copy-start.3 = (f32[2,8]{1,0:T(2,128)S(1)}, f32[2,8]{1,0:T(2,128)}, u32[]{:S(2)}) copy-start(f32[2,8]{1,0:T(2,128)} %table_ref.1) | copy-start | bytes 196
  0.6 0.8 %copy-start.4 = (s32[2]{0:T(128)S(1)}, s32[2]{0:T(128)}, u32[]{:S(2)}) copy-start(s32[2]{0:T(128)} %counts_ref.1) | copy-start | bytes 28
  1.5 0.9 %copy-start = (f32[1,3,8,2048]{3,2,1,0:T(8,128)S(1)}, f32[1,3,8,2048]{3,2,1,0:T(8,128)}, u32[]{:S(2)}) copy-start(f32[1,3,8,2048]{3,2,1,0:T(8,128)} %param.10) | copy-start | bytes 589828
  2.4 0.9 %copy-start.1 = (f32[1,3,8,2048]{3,2,1,0:T(8,128)S(1)}, f32[1,3,8,2048]{3,2,1,0:T(8,128)}, u32[]{:S(2)}) copy-start(f32[1,3,8,2048]{3,2,1,0:T(8,128)} %param.11) | copy-start | bytes 589828
  3.3 0.8 %copy-start.2 = (s32[8,2048]{1,0:T(8,128)S(1)}, s32[8,2048]{1,0:T(8,128)}, u32[]{:S(2)}) copy-start(s32[8,2048]{1,0:T(8,128)} %depth_ref.1) | copy-start | bytes 196612

commit v2 on v1

--- a/solution.py
+++ b/solution.py
@@ -11,9 +11,10 @@
 fine_rate = 0.05
 LANES = 128
 HALF = LANES // 2
+RIM = 16
 MESH = pl.DeviceIdType.MESH
-BLOCK = 2
-GRAD_BLOCK = 2
+BLOCK = 4
+GRAD_BLOCK = 8
 
 
 def kernel(
@@ -48,36 +49,38 @@
     lane = lax.broadcasted_iota(jnp.int32, (8, LANES), 1)
     sub = lax.broadcasted_iota(jnp.int32, (8, LANES), 0)
 
-    def fields_of(ref, start):
-        return ref[:, :, pl.ds(pl.multiple_of(start, LANES), LANES)]
-
     def pack(target, ref, worker, with_depth):
         first = worker * width
         after = jnp.minimum(first + width, cols - LANES)
         before = jnp.maximum(first - LANES, 0)
         right_in = worker < workers - 1
         left_in = worker > 0
-        low = lane < HALF
-        for t in range(own_tiles):
-            target[pl.ds(0, 3), t] = fields_of(ref, first + t * LANES)
-        right = jnp.where(right_in, fields_of(ref, after), 0.0)
-        left = jnp.where(left_in, fields_of(ref, before), 0.0)
-        target[pl.ds(0, 3), own_tiles] = jnp.where(low, right, left)
-        if with_depth:
-            def depth_at(start):
-                at = pl.ds(pl.multiple_of(start, LANES), LANES)
-                return depth_ref[:, at].astype(jnp.float32)
-
+        def depth_at(start):
+            at = pl.ds(pl.multiple_of(start, LANES), LANES)
+            return depth_ref[:, at].astype(jnp.float32)
+
+        def tile_at(f, start):
+            if f == 3:
+                return depth_at(start)
+            return ref[f, :, pl.ds(pl.multiple_of(start, LANES), LANES)]
+
+        count = 4 if with_depth else 3
+        rims = None
+        for f in range(count):
             for t in range(own_tiles):
-                target[3, t] = depth_at(first + t * LANES)
-            target[3, own_tiles] = jnp.where(low, depth_at(after), depth_at(before))
+                target[f * own_tiles + t] = tile_at(f, first + t * LANES)
+            right = jnp.where(right_in, tile_at(f, after), 0.0)
+            left = jnp.where(left_in, tile_at(f, before), 0.0)
+            both = pltpu.roll(jnp.where(lane < HALF, right, left), (2 * f + 1) * RIM % LANES, 1)
+            rims = both if rims is None else jnp.where(lane < 2 * RIM * f, rims, both)
+        target[count * own_tiles] = rims
 
     my_rows = pl.ds(pl.multiple_of(me * strip, strip), strip)
 
     def outward(buffer, landing, sends, receives, k):
         return pltpu.make_async_remote_copy(
             src_ref=buffer.at[k],
-            dst_ref=landing.at[:, :, my_rows, :],
+            dst_ref=landing.at[:, my_rows, :],
             send_sem=sends.at[k],
             recv_sem=receives.at[k],
             device_id={"space": lax.rem(me + k, n)},
@@ -92,8 +95,8 @@
     for k in range(1, n):
         pack(send_state.at[k], state_ref, lax.rem(me + k, n) // share, False)
         outward(send_state, recv_state, state_send, state_recv, k).start()
-    pack(recv_adj.at[:, :, my_rows, :], adjoint_ref, my_worker, True)
-    pack(recv_state.at[:, :, my_rows, :], state_ref, my_worker, False)
+    pack(recv_adj.at[:, my_rows, :], adjoint_ref, my_worker, True)
+    pack(recv_state.at[:, my_rows, :], state_ref, my_worker, False)
 
     total = jnp.where(last, counts_ref[slices - 1], counts_ref[0])
     for s in range(1, slices - 1):
@@ -136,7 +139,12 @@
             ref[c, lead + 1] = jnp.where(sub_wide == 7, 0.0, pltpu.roll(ref[c, 1], 7, 0))
 
     def arrive(landing, field, i):
-        return [landing[field, t, pl.ds(i, 8, stride=lead), :] for t in range(tiles)]
+        at = pl.ds(i, 8, stride=lead)
+        found = [landing[field * own_tiles + t, at, :] for t in range(own_tiles)]
+        rims = landing[landing.shape[0] - 1, at, :]
+        rims = pltpu.roll(rims, (LANES - (2 * field + 1) * RIM) % LANES, 1)
+        near = (lane < RIM) | (lane >= LANES - RIM)
+        return found + [jnp.where(near, rims, 0.0)]
 
     def spread(landing, target):
         def row(i, carry):
@@ -444,10 +452,10 @@
         in_specs=[vmem, smem, smem, smem, vmem, vmem],
         out_specs=(vmem, vmem),
         scratch_shapes=[
-            pltpu.VMEM((n, 4, tiles, strip, LANES), f32),
-            pltpu.VMEM((n, 3, tiles, strip, LANES), f32),
-            pltpu.VMEM((4, tiles, rows, LANES), f32),
-            pltpu.VMEM((3, tiles, rows, LANES), f32),
+            pltpu.VMEM((n, 4 * tiles - 3, strip, LANES), f32),
+            pltpu.VMEM((n, 3 * tiles - 2, strip, LANES), f32),
+            pltpu.VMEM((4 * tiles - 3, rows, LANES), f32),
+            pltpu.VMEM((3 * tiles - 2, rows, LANES), f32),
             pltpu.VMEM((1, lead + 2, 8, span), f32),
             pltpu.VMEM((lead, 8, span), f32),
             pltpu.VMEM((lead, 8, span), f32),

time: 68.4 us -> 55.6 us (0.81)
  Pallas kernels: 62.5 us -> 49.6 us
    pallas_call x1, Pallas kernels: 62.5 us -> 49.6 us  [body(): pl.pallas_call(functools.partial(kernel, geo), out_shape=(jax.ShapeDtypeS...]
where the time goes in v2:
time: 55.6 us; the launch traced here: 55.3 us
  Pallas kernels  49.6 us (89%)
  local copies, waits for them, and re-layouts  5 us (9%)
  between operations  0.68 us (1%)
    pallas_call x1, Pallas kernels, body(): pl.pallas_call(functools.partial(kernel, geo), out_shape=(jax.ShapeDtypeS...  49.6 us
    unnamed x13, local copies, waits for them, and re-layouts  4.88 us

profile of v2, /device:TPU:0, one launch (start us, length us, event | category | flops | bytes accessed | tf_op | source)
XLA Modules:
  0.0 55.3 jit_solution(10316091182485833891)
XLA Ops:
  0.6 0.0 copy-start.3
  0.6 0.0 copy-start.4
  0.7 0.8 %copy.10.weights_ref = f32[9,3,3]{2,1,0:T(4,128)S(1)} copy(f32[9,3,3]{0,2,1:T(4,128)} %param.9) | data formatting | bytes 648 | tf_op args[3]
  1.5 0.0 copy-done.3
  1.5 0.0 copy-done.4
  1.5 0.0 copy-start
  1.5 0.9 %copy-done = f32[1,3,8,2048]{3,2,1,0:T(8,128)S(1)} copy-done((f32[1,3,8,2048]{3,2,1,0:T(8,128)S(1)}, f32[1,3,8,2048]{3,2,1,0:T(8,128)}, u32[]{:S(2)}) %copy-start) | copy-done | bytes 196632
  2.4 0.0 copy-start.1
  2.4 0.9 %copy-done.1 = f32[1,3,8,2048]{3,2,1,0:T(8,128)S(1)} copy-done((f32[1,3,8,2048]{3,2,1,0:T(8,128)S(1)}, f32[1,3,8,2048]{3,2,1,0:T(8,128)}, u32[]{:S(2)}) %copy-start.1) | copy-done | bytes 196632
  3.3 0.0 copy-start.2
  3.3 0.8 %copy-done.2 = s32[8,2048]{1,0:T(8,128)S(1)} copy-done((s32[8,2048]{1,0:T(8,128)S(1)}, s32[8,2048]{1,0:T(8,128)}, u32[]{:S(2)}) %copy-start.2) | copy-done | bytes 65560
  4.2 49.6 %shard_map.77 = (f32[1,3,8,2048]{3,2,1,0:T(8,128)S(1)}, f32[8,128]{1,0:T(8,128)S(1)}) custom-call(s32[8,2048]{1,0:T(8,128)S(1)} %copy-done.2, f32[2,8]{1,0:T(2,128)S(1)} %copy-done.3, s32[2]{0:T(128)S(1)} %copy-done.4, f32[9,3,3]{2,1,0:T(4,128)S(1)} %copy.10.weights_ref, f32[3,8,2048]{2,1,0:T(8,128)S(1)} %bitcast.2, f32[3,8,2048]{2,1,0:T(8,128)S(1)} %bitcast.3), custom_call_target="tpu_custom_call" | custom-call | tf_op jit(solution)/shard_map/pallas_call | solution.py:446
  53.8 0.1 reshape_squeeze.3
  53.9 0.7 %copy.11 = f32[9,3,3]{0,2,1:T(4,128)} copy(f32[9,3,3]{2,1,0:T(4,128)S(1)} %reshape_squeeze.3) | data formatting | bytes 648
  54.6 0.7 %copy.13 = f32[1,3,8,2048]{3,2,1,0:T(8,128)} copy(f32[1,3,8,2048]{3,2,1,0:T(8,128)S(1)} %get-tuple-element.12) | data formatting | bytes 393216
  (1 shorter events, 0.0 us)
Async XLA Ops:
  0.6 0.8 %copy-start.3 = (f32[2,8]{1,0:T(2,128)S(1)}, f32[2,8]{1,0:T(2,128)}, u32[]{:S(2)}) copy-start(f32[2,8]{1,0:T(2,128)} %table_ref.1) | copy-start | bytes 196
  0.6 0.8 %copy-start.4 = (s32[2]{0:T(128)S(1)}, s32[2]{0:T(128)}, u32[]{:S(2)}) copy-start(s32[2]{0:T(128)} %counts_ref.1) | copy-start | bytes 28
  1.5 0.9 %copy-start = (f32[1,3,8,2048]{3,2,1,0:T(8,128)S(1)}, f32[1,3,8,2048]{3,2,1,0:T(8,128)}, u32[]{:S(2)}) copy-start(f32[1,3,8,2048]{3,2,1,0:T(8,128)} %param.10) | copy-start | bytes 589828
  2.4 0.9 %copy-start.1 = (f32[1,3,8,2048]{3,2,1,0:T(8,128)S(1)}, f32[1,3,8,2048]{3,2,1,0:T(8,128)}, u32[]{:S(2)}) copy-start(f32[1,3,8,2048]{3,2,1,0:T(8,128)} %param.11) | copy-start | bytes 589828
  3.3 0.8 %copy-start.2 = (s32[8,2048]{1,0:T(8,128)S(1)}, s32[8,2048]{1,0:T(8,128)}, u32[]{:S(2)}) copy-start(s32[8,2048]{1,0:T(8,128)} %depth_ref.1) | copy-start | bytes 196612

commit v3 on v2

--- a/solution.py
+++ b/solution.py
@@ -13,7 +13,7 @@
 HALF = LANES // 2
 RIM = 16
 MESH = pl.DeviceIdType.MESH
-BLOCK = 4
+BLOCK = 8
 GRAD_BLOCK = 8
 
 

time: 55.6 us -> 54.3 us (0.977)
  Pallas kernels: 49.6 us -> 48.3 us
    pallas_call x1, Pallas kernels: 49.6 us -> 48.3 us  [body(): pl.pallas_call(functools.partial(kernel, geo), out_shape=(jax.ShapeDtypeS...]
where the time goes in v3:
time: 54.3 us; the launch traced here: 54 us
  Pallas kernels  48.3 us (89%)
  local copies, waits for them, and re-layouts  5 us (9%)
  between operations  0.68 us (1%)
    pallas_call x1, Pallas kernels, body(): pl.pallas_call(functools.partial(kernel, geo), out_shape=(jax.ShapeDtypeS...  48.3 us
    unnamed x13, local copies, waits for them, and re-layouts  4.88 us

profile of v3, /device:TPU:0, one launch (start us, length us, event | category | flops | bytes accessed | tf_op | source)
XLA Modules:
  0.0 54.0 jit_solution(10547053306618784680)
XLA Ops:
  0.6 0.0 copy-start.3
  0.6 0.0 copy-start.4
  0.7 0.8 %copy.10.weights_ref = f32[9,3,3]{2,1,0:T(4,128)S(1)} copy(f32[9,3,3]{0,2,1:T(4,128)} %param.9) | data formatting | bytes 648 | tf_op args[3]
  1.5 0.0 copy-done.3
  1.5 0.0 copy-done.4
  1.5 0.0 copy-start
  1.5 0.9 %copy-done = f32[1,3,8,2048]{3,2,1,0:T(8,128)S(1)} copy-done((f32[1,3,8,2048]{3,2,1,0:T(8,128)S(1)}, f32[1,3,8,2048]{3,2,1,0:T(8,128)}, u32[]{:S(2)}) %copy-start) | copy-done | bytes 196632
  2.4 0.0 copy-start.1
  2.4 0.9 %copy-done.1 = f32[1,3,8,2048]{3,2,1,0:T(8,128)S(1)} copy-done((f32[1,3,8,2048]{3,2,1,0:T(8,128)S(1)}, f32[1,3,8,2048]{3,2,1,0:T(8,128)}, u32[]{:S(2)}) %copy-start.1) | copy-done | bytes 196632
  3.3 0.0 copy-start.2
  3.3 0.8 %copy-done.2 = s32[8,2048]{1,0:T(8,128)S(1)} copy-done((s32[8,2048]{1,0:T(8,128)S(1)}, s32[8,2048]{1,0:T(8,128)}, u32[]{:S(2)}) %copy-start.2) | copy-done | bytes 65560
  4.2 48.3 %shard_map.77 = (f32[1,3,8,2048]{3,2,1,0:T(8,128)S(1)}, f32[8,128]{1,0:T(8,128)S(1)}) custom-call(s32[8,2048]{1,0:T(8,128)S(1)} %copy-done.2, f32[2,8]{1,0:T(2,128)S(1)} %copy-done.3, s32[2]{0:T(128)S(1)} %copy-done.4, f32[9,3,3]{2,1,0:T(4,128)S(1)} %copy.10.weights_ref, f32[3,8,2048]{2,1,0:T(8,128)S(1)} %bitcast.2, f32[3,8,2048]{2,1,0:T(8,128)S(1)} %bitcast.3), custom_call_target="tpu_custom_call" | custom-call | tf_op jit(solution)/shard_map/pallas_call | solution.py:446
  52.5 0.1 reshape_squeeze.3
  52.6 0.7 %copy.11 = f32[9,3,3]{0,2,1:T(4,128)} copy(f32[9,3,3]{2,1,0:T(4,128)S(1)} %reshape_squeeze.3) | data formatting | bytes 648
  53.3 0.7 %copy.13 = f32[1,3,8,2048]{3,2,1,0:T(8,128)} copy(f32[1,3,8,2048]{3,2,1,0:T(8,128)S(1)} %get-tuple-element.12) | data formatting | bytes 393216
  (1 shorter events, 0.0 us)
Async XLA Ops:
  0.6 0.8 %copy-start.3 = (f32[2,8]{1,0:T(2,128)S(1)}, f32[2,8]{1,0:T(2,128)}, u32[]{:S(2)}) copy-start(f32[2,8]{1,0:T(2,128)} %table_ref.1) | copy-start | bytes 196
  0.6 0.8 %copy-start.4 = (s32[2]{0:T(128)S(1)}, s32[2]{0:T(128)}, u32[]{:S(2)}) copy-start(s32[2]{0:T(128)} %counts_ref.1) | copy-start | bytes 28
  1.5 0.9 %copy-start = (f32[1,3,8,2048]{3,2,1,0:T(8,128)S(1)}, f32[1,3,8,2048]{3,2,1,0:T(8,128)}, u32[]{:S(2)}) copy-start(f32[1,3,8,2048]{3,2,1,0:T(8,128)} %param.10) | copy-start | bytes 589828
  2.4 0.9 %copy-start.1 = (f32[1,3,8,2048]{3,2,1,0:T(8,128)S(1)}, f32[1,3,8,2048]{3,2,1,0:T(8,128)}, u32[]{:S(2)}) copy-start(f32[1,3,8,2048]{3,2,1,0:T(8,128)} %param.11) | copy-start | bytes 589828
  3.3 0.8 %copy-start.2 = (s32[8,2048]{1,0:T(8,128)S(1)}, s32[8,2048]{1,0:T(8,128)}, u32[]{:S(2)}) copy-start(s32[8,2048]{1,0:T(8,128)} %depth_ref.1) | copy-start | bytes 196612
